TPU v7x, 128 devices: a whole 4x4x4 slice. The times are simulated.
128 devices in a mesh: pipe: 2 (over core), ctx: 16 (over y, x), dp: 4 (over z).
Axes of the slice: x: 4, y: 4, z: 4, core: 2. Of those that a mesh axis runs over, the one named last changes fastest.
Arguments:
- queries: bfloat16 [2, 4, 2048, 2048], P('pipe', 'dp', 'ctx'), may hold values from -16 to 16
- key_rows: bfloat16 [2, 4, 2048, 512], P('pipe', 'dp', 'ctx'), may hold values from -8 to 8
- layer_value_rows: bfloat16 [2, 4, 2048, 512], P('pipe', 'dp', 'ctx'), may hold values from -6 to 6
- prior_output: bfloat16 [2, 4, 2048, 2048], P('pipe', 'dp', 'ctx'), may hold values from -3 to 3
- later_grad: bfloat16 [2, 4, 2048, 2048], P('pipe', 'dp', 'ctx'), may hold values from -6 to 6
- block_order: int32 [32], replicated, may hold values from 0 to 31, each once
- log_table: float32 [2, 16], P('pipe'), may hold values from 0 to 3
- dim_index: int32 [2, 64], P('pipe'), may hold values from 0 to 15, as said below
Outputs:
- attended: bfloat16 [2, 4, 2048, 2048], P('pipe', 'dp', 'ctx')
- query_gradient: bfloat16 [2, 4, 2048, 2048], P('pipe', 'dp', 'ctx')
- key_gradient: bfloat16 [2, 4, 2048, 512], P('pipe', 'dp', 'ctx')
- value_gradient: bfloat16 [2, 4, 2048, 512], P('pipe', 'dp', 'ctx')
- table_grad: float32 [2, 16], P('pipe')
Inputs may be any that keep to these rules, and one draw needn't show every extreme that they name: `block_order`: a permutation. `dim_index`: each row names every table entry equally often.
All inputs are finite; a program needn't handle non-finite values.
Results may differ from a plain program's by a relative error of at most 0.025.
Values may be sent and summed in bfloat16 or wider, within the bound.
No kernel may reach another device: no remote copies, remote signals or barrier semaphores. Data moves between devices by JAX's collectives and lax.ppermute only.
A program may use at most 64 MiB of HBM per device.

v0:
```python
import jax
import jax.numpy as jnp
from jax import lax
from jax.sharding import PartitionSpec as P

HEAD_SIZE = 128
neg_large = -1e30
rope_base = 500000.0


def passed_along(value, axis, by):
    size = lax.axis_size(axis)
    return lax.ppermute(value, axis, [(i, (i + by) % size) for i in range(size)])


def apply_rotation(vectors, cosine_values, sine_lookup):
    half_len = vectors.shape[-1] // 2
    lower_half = vectors[..., :half_len]
    upper_half = vectors[..., half_len:]
    return jnp.concatenate(
        [
            lower_half * cosine_values - upper_half * sine_lookup,
            lower_half * sine_lookup + upper_half * cosine_values,
        ],
        axis=-1,
    )


def rotate_back(gradient, cosine_values, sine_lookup):
    half_len = gradient.shape[-1] // 2
    lower_half = gradient[..., :half_len]
    upper_half = gradient[..., half_len:]
    return jnp.concatenate(
        [
            lower_half * cosine_values + upper_half * sine_lookup,
            upper_half * cosine_values - lower_half * sine_lookup,
        ],
        axis=-1,
    )


def angle_grad(gradient, rotated):
    half_len = gradient.shape[-1] // 2
    return jnp.sum(
        gradient[..., half_len:] * rotated[..., :half_len]
        - gradient[..., :half_len] * rotated[..., half_len:],
        axis=1,
    )


def angles_for(table_row, index_row, positions, head_dim):
    half_len = head_dim // 2
    onehot = (
        index_row[:, None] == jnp.arange(table_row.shape[0], dtype=jnp.int32)[None, :]
    ).astype(jnp.float32)
    log_factor = jnp.dot(onehot, table_row, precision=lax.Precision.HIGHEST)
    base_rate = rope_base ** (-(jnp.arange(half_len, dtype=jnp.float32) * 2.0 / head_dim))
    scaled_rate = base_rate * jnp.exp(-log_factor)
    return (onehot, positions[:, None] * scaled_rate[None, :])


def slot_positions(block_order, device, tok_rows):
    half_len = tok_rows // 2
    blocks = lax.dynamic_slice_in_dim(block_order, device * 2, 2)
    return (
        (blocks[:, None] * half_len + jnp.arange(half_len, dtype=jnp.int32)[None, :])
        .reshape(-1)
        .astype(jnp.float32)
    )


def on_device(
    queries, key_rows, layer_value_rows, prior_output, later_grad, block_order, log_table, dim_index
):
    tok_rows = queries.shape[2]
    q_width = queries.shape[3]
    kv_width = key_rows.shape[3]
    kv_heads = kv_width // HEAD_SIZE
    group_size = q_width // kv_width
    cycle_size = lax.axis_size("ctx")
    my_index = lax.axis_index("ctx")
    score_scale = HEAD_SIZE ** (-0.5)
    arriving = passed_along(prior_output, "pipe", 1)
    returning = passed_along(later_grad, "pipe", -1)
    positions = slot_positions(block_order, my_index, tok_rows)
    onehot, angles = angles_for(log_table[0], dim_index[0], positions, HEAD_SIZE)
    cosine_values = jnp.cos(angles)[:, None, :]
    sine_lookup = jnp.sin(angles)[:, None, :]
    mixed = (queries[0, 0].astype(jnp.float32) + arriving[0, 0].astype(jnp.float32)).reshape(
        tok_rows, kv_heads * group_size, HEAD_SIZE
    )
    rotated_query_rows = apply_rotation(mixed, cosine_values, sine_lookup).astype(jnp.bfloat16)
    rotated_key_rows = apply_rotation(
        key_rows[0, 0].astype(jnp.float32).reshape(tok_rows, kv_heads, HEAD_SIZE),
        cosine_values,
        sine_lookup,
    ).astype(jnp.bfloat16)
    grouped_queries = rotated_query_rows.reshape(tok_rows, kv_heads, group_size, HEAD_SIZE)
    value_head_rows = layer_value_rows[0, 0].reshape(tok_rows, kv_heads, HEAD_SIZE)
    output_gradient = returning[0, 0].reshape(tok_rows, kv_heads, group_size, HEAD_SIZE)
    key_value = jnp.stack([rotated_key_rows, value_head_rows])

    def visit(softmax_state, block_pair, key_pos):
        maxima, totals, accumulated = softmax_state
        scores = (
            jnp.einsum(
                "qhgd,khd->hgqk", grouped_queries, block_pair[0], preferred_element_type=jnp.float32
            )
            * score_scale
        )
        visible = key_pos[None, :] <= positions[:, None]
        row_max = jnp.max(jnp.where(visible, scores, neg_large), axis=-1)
        new_max = jnp.maximum(maxima, row_max)
        weights = jnp.where(visible, jnp.exp(scores - new_max[..., None]), 0.0)
        rescale = jnp.exp(maxima - new_max)
        totals = totals * rescale + jnp.sum(weights, axis=-1)
        summed = jnp.einsum(
            "hgqk,khd->qhgd",
            weights.astype(jnp.bfloat16),
            block_pair[1],
            preferred_element_type=jnp.float32,
        )
        accumulated = accumulated * jnp.moveaxis(rescale, -1, 0)[..., None] + summed
        return (new_max, totals, accumulated)

    def visit_back(block_pair, key_pos, log_totals, row_delta):
        scores = (
            jnp.einsum(
                "qhgd,khd->hgqk", grouped_queries, block_pair[0], preferred_element_type=jnp.float32
            )
            * score_scale
        )
        visible = key_pos[None, :] <= positions[:, None]
        probs = jnp.where(visible, jnp.exp(scores - log_totals[..., None]), 0.0)
        value_part = jnp.einsum(
            "hgqk,qhgd->khd",
            probs.astype(jnp.bfloat16),
            output_gradient,
            preferred_element_type=jnp.float32,
        )
        prob_grad = jnp.einsum(
            "qhgd,khd->hgqk", output_gradient, block_pair[1], preferred_element_type=jnp.float32
        )
        score_grad = (probs * (prob_grad - row_delta[..., None])).astype(jnp.bfloat16)
        query_part = jnp.einsum(
            "hgqk,khd->qhgd", score_grad, block_pair[0], preferred_element_type=jnp.float32
        )
        key_part = jnp.einsum(
            "hgqk,qhgd->khd", score_grad, grouped_queries, preferred_element_type=jnp.float32
        )
        return (query_part, jnp.stack([key_part, value_part]))

    initial = (
        jnp.full((kv_heads, group_size, tok_rows), neg_large, jnp.float32),
        jnp.zeros((kv_heads, group_size, tok_rows), jnp.float32),
        jnp.zeros((tok_rows, kv_heads, group_size, HEAD_SIZE), jnp.float32),
    )

    def guarded(softmax_state, block_pair, key_pos):
        return lax.cond(
            jnp.min(key_pos) <= jnp.max(positions),
            lambda held: visit(held, block_pair, key_pos),
            lambda held: held,
            softmax_state,
        )

    empty_query = jnp.zeros((tok_rows, kv_heads, group_size, HEAD_SIZE), jnp.float32)
    empty_pair = jnp.zeros((2, tok_rows, kv_heads, HEAD_SIZE), jnp.float32)

    def back_terms(block_pair, key_pos, log_totals, row_delta):
        return lax.cond(
            jnp.min(key_pos) <= jnp.max(positions),
            lambda held: visit_back(held, key_pos, log_totals, row_delta),
            lambda held: (empty_query, empty_pair),
            block_pair,
        )

    def forward_turn(turn_index, carried):
        softmax_state, block_pair = carried
        source = (my_index - turn_index) % cycle_size
        softmax_state = guarded(
            softmax_state, block_pair, slot_positions(block_order, source, tok_rows)
        )
        block_pair = passed_along(block_pair, "ctx", 1)
        return (softmax_state, block_pair)

    softmax_state, block_pair = lax.fori_loop(0, cycle_size - 1, forward_turn, (initial, key_value))
    last_source = (my_index + 1) % cycle_size
    softmax_state = guarded(
        softmax_state, block_pair, slot_positions(block_order, last_source, tok_rows)
    )
    maxima, totals, accumulated = softmax_state
    final_result = (accumulated / jnp.moveaxis(totals, -1, 0)[..., None]).astype(jnp.bfloat16)
    finish_log_totals = maxima + jnp.log(totals)
    finish_row_delta = jnp.moveaxis(
        jnp.sum(output_gradient.astype(jnp.float32) * final_result.astype(jnp.float32), axis=-1),
        0,
        -1,
    )
    final_result, log_totals, row_delta = (final_result, finish_log_totals, finish_row_delta)

    def backward_turn(turn_index, carried):
        query_sum, block_pair, travel_grads = carried
        source = (my_index - turn_index) % cycle_size
        key_pos = slot_positions(block_order, source, tok_rows)
        query_part, pair_part = back_terms(block_pair, key_pos, log_totals, row_delta)
        query_sum = query_sum + query_part
        travel_grads = travel_grads + pair_part
        block_pair = passed_along(block_pair, "ctx", 1)
        travel_grads = passed_along(travel_grads.astype(jnp.bfloat16), "ctx", 1).astype(
            travel_grads.dtype
        )
        return (query_sum, block_pair, travel_grads)

    query_sum, block_pair, own_grads = lax.fori_loop(
        0, cycle_size, backward_turn, (empty_query, key_value, empty_pair)
    )
    query_rot_grad = (query_sum * score_scale).reshape(tok_rows, kv_heads * group_size, HEAD_SIZE)
    key_rot_grad = own_grads[0] * score_scale
    query_gradient = rotate_back(query_rot_grad, cosine_values, sine_lookup).astype(jnp.bfloat16)
    key_gradient = rotate_back(key_rot_grad, cosine_values, sine_lookup).astype(jnp.bfloat16)
    value_gradient = own_grads[1].astype(jnp.bfloat16)
    angle_sums = angle_grad(query_rot_grad, rotated_query_rows.astype(jnp.float32)) + angle_grad(
        key_rot_grad, rotated_key_rows.astype(jnp.float32)
    )
    log_gradient = -jnp.sum(angle_sums * angles, axis=0)
    partial_value = jnp.dot(log_gradient, onehot, precision=lax.Precision.HIGHEST)
    summed_table = lax.psum(partial_value, ("ctx", "dp"))
    table_grad = summed_table / (cycle_size * lax.axis_size("dp") * tok_rows)
    return (
        final_result.reshape(1, 1, tok_rows, q_width),
        query_gradient.reshape(1, 1, tok_rows, q_width),
        key_gradient.reshape(1, 1, tok_rows, kv_width),
        value_gradient.reshape(1, 1, tok_rows, kv_width),
        table_grad[None, :],
    )


def solution(mesh):
    placed = (
        P("pipe", "dp", "ctx", None),
        P("pipe", "dp", "ctx", None),
        P("pipe", "dp", "ctx", None),
        P("pipe", "dp", "ctx", None),
        P("pipe", "dp", "ctx", None),
        P(),
        P("pipe", None),
        P("pipe", None),
    )
    return jax.shard_map(
        on_device,
        mesh=mesh,
        in_specs=placed,
        out_specs=(
            P("pipe", "dp", "ctx", None),
            P("pipe", "dp", "ctx", None),
            P("pipe", "dp", "ctx", None),
            P("pipe", "dp", "ctx", None),
            P("pipe", None),
        ),
        check_vma=False,
    )
```

profile of v0, /device:TPU:0, one launch (start us, length us, event | category | flops | bytes accessed | tf_op | source)
XLA Modules:
  0.0 693.5 jit_solution(15029671179001092386)
XLA Ops:
  14.0 171.1 %while.42 = (s32[]{:T(128)}, f32[4,4,128]{2,1,0:T(4,128)S(1)}, f32[4,4,128]{2,1,0:T(4,128)S(1)}, f32[128,4,4,128]{3,0,2,1:T(8,128)S(1)}, bf16[2,128,4,128]{3,1,2...) while((s32[]{:T(128)}, f32[4,4,128]{2,1,0:T(4,128)S(1)}, ...), condition=%wide.region_8.9_spmd.clone, body=%wide.region_2.8_spmd.clone.sunk | while | flops 137124752 | bytes 7803410 | solution.py:187
  32.8 5.8 collective-permute-done
  52.4 7.8 %collective-permute-done = bf16[2,128,4,128]{3,1,2,0:T(8,128)(2,1)S(1)} collective-permute-done((bf16[2,128,4,128]{3,1,2,0:T(8,128)(2,1)}, bf16[2,128,4,128]{3,1,2,0:T(8,128)(2,1)S(1)}, u32[]{:S(2)}, u32[]{:S(2)}) %collective-permute-start) | collective-permute-done | bytes 262176 | tf_op jit(solution)/shard_map/while/body/eval_jaxpr/ppermute | solution.py:13
  98.3 5.7 collective-permute-done
  110.1 6.9 collective-permute-done
  123.1 6.6 collective-permute-done
  135.8 5.7 collective-permute-done
  192.8 315.9 %while.43 = (s32[]{:T(128)}, f32[128,4,4,128]{3,0,2,1:T(8,128)}, bf16[2,128,4,128]{3,1,2,0:T(8,128)(2,1)S(1)}, f32[2,128,4,128]{3,1,2,0:T(8,128)S(1)}, s32[]{:T(...) while((s32[]{:T(128)}, f32[128,4,4,128]{3,0,2,1:T(8,128)}, ...), condition=%wide.region_18.19_spmd.clone, body=%wide.region_14.0_spmd.clone.sunk | while | flops 338576288 | bytes 17750600 | solution.py:215
  203.3 10.5 %collective-permute-done.2 = bf16[2,128,4,128]{3,1,2,0:T(8,128)(2,1)S(1)} collective-permute-done((bf16[2,128,4,128]{3,1,2,0:T(8,128)(2,1)}, bf16[2,128,4,128]{3,1,2,0:T(8,128)(2,1)S(1)}, u32[]{:S(2)}, u32[]{:S(2)}) %collective-permute-start.2) | collective-permute-done | bytes 262176 | tf_op jit(solution)/shard_map/while/body/eval_jaxpr/ppermute | solution.py:13
  217.0 5.3 conditional.9
  225.5 10.2 %collective-permute-done.2 = bf16[2,128,4,128]{3,1,2,0:T(8,128)(2,1)S(1)} collective-permute-done((bf16[2,128,4,128]{3,1,2,0:T(8,128)(2,1)}, bf16[2,128,4,128]{3,1,2,0:T(8,128)(2,1)S(1)}, u32[]{:S(2)}, u32[]{:S(2)}) %collective-permute-start.2) | collective-permute-done | bytes 262176 | tf_op jit(solution)/shard_map/while/body/eval_jaxpr/ppermute | solution.py:13
  239.0 5.3 conditional.9
  247.5 9.4 %collective-permute-done.2 = bf16[2,128,4,128]{3,1,2,0:T(8,128)(2,1)S(1)} collective-permute-done((bf16[2,128,4,128]{3,1,2,0:T(8,128)(2,1)}, bf16[2,128,4,128]{3,1,2,0:T(8,128)(2,1)S(1)}, u32[]{:S(2)}, u32[]{:S(2)}) %collective-permute-start.2) | collective-permute-done | bytes 262176 | tf_op jit(solution)/shard_map/while/body/eval_jaxpr/ppermute | solution.py:13
  263.5 13.6 %collective-permute-done.2 = bf16[2,128,4,128]{3,1,2,0:T(8,128)(2,1)S(1)} collective-permute-done((bf16[2,128,4,128]{3,1,2,0:T(8,128)(2,1)}, bf16[2,128,4,128]{3,1,2,0:T(8,128)(2,1)S(1)}, u32[]{:S(2)}, u32[]{:S(2)}) %collective-permute-start.2) | collective-permute-done | bytes 262176 | tf_op jit(solution)/shard_map/while/body/eval_jaxpr/ppermute | solution.py:13
  280.5 5.3 conditional.9
  288.9 7.6 %collective-permute-done.2 = bf16[2,128,4,128]{3,1,2,0:T(8,128)(2,1)S(1)} collective-permute-done((bf16[2,128,4,128]{3,1,2,0:T(8,128)(2,1)}, bf16[2,128,4,128]{3,1,2,0:T(8,128)(2,1)S(1)}, u32[]{:S(2)}, u32[]{:S(2)}) %collective-permute-start.2) | collective-permute-done | bytes 262176 | tf_op jit(solution)/shard_map/while/body/eval_jaxpr/ppermute | solution.py:13
  308.3 7.5 %collective-permute-done.2 = bf16[2,128,4,128]{3,1,2,0:T(8,128)(2,1)S(1)} collective-permute-done((bf16[2,128,4,128]{3,1,2,0:T(8,128)(2,1)}, bf16[2,128,4,128]{3,1,2,0:T(8,128)(2,1)S(1)}, u32[]{:S(2)}, u32[]{:S(2)}) %collective-permute-start.2) | collective-permute-done | bytes 262176 | tf_op jit(solution)/shard_map/while/body/eval_jaxpr/ppermute | solution.py:13
  319.1 5.3 conditional.9
  327.6 7.5 %collective-permute-done.2 = bf16[2,128,4,128]{3,1,2,0:T(8,128)(2,1)S(1)} collective-permute-done((bf16[2,128,4,128]{3,1,2,0:T(8,128)(2,1)}, bf16[2,128,4,128]{3,1,2,0:T(8,128)(2,1)S(1)}, u32[]{:S(2)}, u32[]{:S(2)}) %collective-permute-start.2) | collective-permute-done | bytes 262176 | tf_op jit(solution)/shard_map/while/body/eval_jaxpr/ppermute | solution.py:13
  346.9 7.5 %collective-permute-done.2 = bf16[2,128,4,128]{3,1,2,0:T(8,128)(2,1)S(1)} collective-permute-done((bf16[2,128,4,128]{3,1,2,0:T(8,128)(2,1)}, bf16[2,128,4,128]{3,1,2,0:T(8,128)(2,1)S(1)}, u32[]{:S(2)}, u32[]{:S(2)}) %collective-permute-start.2) | collective-permute-done | bytes 262176 | tf_op jit(solution)/shard_map/while/body/eval_jaxpr/ppermute | solution.py:13
  357.7 5.3 conditional.9
  366.1 7.5 %collective-permute-done.2 = bf16[2,128,4,128]{3,1,2,0:T(8,128)(2,1)S(1)} collective-permute-done((bf16[2,128,4,128]{3,1,2,0:T(8,128)(2,1)}, bf16[2,128,4,128]{3,1,2,0:T(8,128)(2,1)S(1)}, u32[]{:S(2)}, u32[]{:S(2)}) %collective-permute-start.2) | collective-permute-done | bytes 262176 | tf_op jit(solution)/shard_map/while/body/eval_jaxpr/ppermute | solution.py:13
  385.4 7.5 %collective-permute-done.2 = bf16[2,128,4,128]{3,1,2,0:T(8,128)(2,1)S(1)} collective-permute-done((bf16[2,128,4,128]{3,1,2,0:T(8,128)(2,1)}, bf16[2,128,4,128]{3,1,2,0:T(8,128)(2,1)S(1)}, u32[]{:S(2)}, u32[]{:S(2)}) %collective-permute-start.2) | collective-permute-done | bytes 262176 | tf_op jit(solution)/shard_map/while/body/eval_jaxpr/ppermute | solution.py:13
  396.2 5.3 conditional.9
  404.7 7.5 %collective-permute-done.2 = bf16[2,128,4,128]{3,1,2,0:T(8,128)(2,1)S(1)} collective-permute-done((bf16[2,128,4,128]{3,1,2,0:T(8,128)(2,1)}, bf16[2,128,4,128]{3,1,2,0:T(8,128)(2,1)S(1)}, u32[]{:S(2)}, u32[]{:S(2)}) %collective-permute-start.2) | collective-permute-done | bytes 262176 | tf_op jit(solution)/shard_map/while/body/eval_jaxpr/ppermute | solution.py:13
  424.0 7.5 %collective-permute-done.2 = bf16[2,128,4,128]{3,1,2,0:T(8,128)(2,1)S(1)} collective-permute-done((bf16[2,128,4,128]{3,1,2,0:T(8,128)(2,1)}, bf16[2,128,4,128]{3,1,2,0:T(8,128)(2,1)S(1)}, u32[]{:S(2)}, u32[]{:S(2)}) %collective-permute-start.2) | collective-permute-done | bytes 262176 | tf_op jit(solution)/shard_map/while/body/eval_jaxpr/ppermute | solution.py:13
  434.8 5.3 conditional.9
  443.2 7.5 %collective-permute-done.2 = bf16[2,128,4,128]{3,1,2,0:T(8,128)(2,1)S(1)} collective-permute-done((bf16[2,128,4,128]{3,1,2,0:T(8,128)(2,1)}, bf16[2,128,4,128]{3,1,2,0:T(8,128)(2,1)S(1)}, u32[]{:S(2)}, u32[]{:S(2)}) %collective-permute-start.2) | collective-permute-done | bytes 262176 | tf_op jit(solution)/shard_map/while/body/eval_jaxpr/ppermute | solution.py:13
  462.5 7.5 %collective-permute-done.2 = bf16[2,128,4,128]{3,1,2,0:T(8,128)(2,1)S(1)} collective-permute-done((bf16[2,128,4,128]{3,1,2,0:T(8,128)(2,1)}, bf16[2,128,4,128]{3,1,2,0:T(8,128)(2,1)S(1)}, u32[]{:S(2)}, u32[]{:S(2)}) %collective-permute-start.2) | collective-permute-done | bytes 262176 | tf_op jit(solution)/shard_map/while/body/eval_jaxpr/ppermute | solution.py:13
  481.8 7.5 %collective-permute-done.2 = bf16[2,128,4,128]{3,1,2,0:T(8,128)(2,1)S(1)} collective-permute-done((bf16[2,128,4,128]{3,1,2,0:T(8,128)(2,1)}, bf16[2,128,4,128]{3,1,2,0:T(8,128)(2,1)S(1)}, u32[]{:S(2)}, u32[]{:S(2)}) %collective-permute-start.2) | collective-permute-done | bytes 262176 | tf_op jit(solution)/shard_map/while/body/eval_jaxpr/ppermute | solution.py:13
  501.1 7.5 %collective-permute-done.2 = bf16[2,128,4,128]{3,1,2,0:T(8,128)(2,1)S(1)} collective-permute-done((bf16[2,128,4,128]{3,1,2,0:T(8,128)(2,1)}, bf16[2,128,4,128]{3,1,2,0:T(8,128)(2,1)S(1)}, u32[]{:S(2)}, u32[]{:S(2)}) %collective-permute-start.2) | collective-permute-done | bytes 262176 | tf_op jit(solution)/shard_map/while/body/eval_jaxpr/ppermute | solution.py:13
  514.5 174.3 %psum.7 = f32[16]{0:T(128)S(1)} all-reduce(f32[16]{0:T(128)S(1)} %convolution_bitcast_fusion.6), channel_id=1, replica_groups=mesh['pipe'=2,'ctx'=16,'dp'=4] {'ctx','dp'}, use_global_device_ids=true, to_apply=%region_22.23 | all-reduce | flops 16 | bytes 128 | tf_op jit(solution)/shard_map/psum | solution.py:228
  (700 shorter events, 397.3 us)
Async XLA Ops:
  0.6 10.1 %collective-permute-start.3 = (bf16[1,1,128,2048]{3,2,1,0:T(8,128)(2,1)}, bf16[1,1,128,2048]{3,2,1,0:T(8,128)(2,1)S(1)}, u32[]{:S(2)}, u32[]{:S(2)}) collective-permute-start(bf16[1,1,128,2048]{3,2,1,0:T(8,128)(2,1)} %param.21), channel_id=1, source_target_pairs={{0,64},{64,0},{1,65},{65,1},{2,66},{66,2},{3,67},{67,3},{4,68},{68... | collective-permute-start | bytes 1572872 | tf_op jit(solution)/shard_map/ppermute | solution.py:13
  2.8 186.4 %collective-permute-start.4 = (bf16[1,1,128,2048]{2,3,1,0:T(8,128)(2,1)}, bf16[1,1,128,2048]{2,3,1,0:T(8,128)(2,1)}, u32[]{:S(2)}, u32[]{:S(2)}) collective-permute-start(bf16[1,1,128,2048]{2,3,1,0:T(8,128)(2,1)} %copy.95), channel_id=1, source_target_pairs={{0,64},{64,0},{1,65},{65,1},{2,66},{66,2},{3,67},{67,3},{4,68},{68... | collective-permute-start | bytes 1572872 | tf_op jit(solution)/shard_map/ppermute | solution.py:13
  14.7 12.0 %collective-permute-start = (bf16[2,128,4,128]{3,1,2,0:T(8,128)(2,1)}, bf16[2,128,4,128]{3,1,2,0:T(8,128)(2,1)S(1)}, u32[]{:S(2)}, u32[]{:S(2)}) collective-permute-start(bf16[2,128,4,128]{3,1,2,0:T(8,128)(2,1)} %copy.144), channel_id=1, source_target_pairs={{0,4},{4,8},{8,12},{12,16},{16,20},{20,24},{24,28},{28,32},{32,36}... | collective-permute-start | bytes 786440 | tf_op jit(solution)/shard_map/while/body/eval_jaxpr/ppermute | solution.py:13
  27.4 11.2 %collective-permute-start = (bf16[2,128,4,128]{3,1,2,0:T(8,128)(2,1)}, bf16[2,128,4,128]{3,1,2,0:T(8,128)(2,1)S(1)}, u32[]{:S(2)}, u32[]{:S(2)}) collective-permute-start(bf16[2,128,4,128]{3,1,2,0:T(8,128)(2,1)} %copy.144), channel_id=1, source_target_pairs={{0,4},{4,8},{8,12},{12,16},{16,20},{20,24},{24,28},{28,32},{32,36}... | collective-permute-start | bytes 786440 | tf_op jit(solution)/shard_map/while/body/eval_jaxpr/ppermute | solution.py:13
  39.3 10.3 %collective-permute-start = (bf16[2,128,4,128]{3,1,2,0:T(8,128)(2,1)}, bf16[2,128,4,128]{3,1,2,0:T(8,128)(2,1)S(1)}, u32[]{:S(2)}, u32[]{:S(2)}) collective-permute-start(bf16[2,128,4,128]{3,1,2,0:T(8,128)(2,1)} %copy.144), channel_id=1, source_target_pairs={{0,4},{4,8},{8,12},{12,16},{16,20},{20,24},{24,28},{28,32},{32,36}... | collective-permute-start | bytes 786440 | tf_op jit(solution)/shard_map/while/body/eval_jaxpr/ppermute | solution.py:13
  92.9 11.1 %collective-permute-start = (bf16[2,128,4,128]{3,1,2,0:T(8,128)(2,1)}, bf16[2,128,4,128]{3,1,2,0:T(8,128)(2,1)S(1)}, u32[]{:S(2)}, u32[]{:S(2)}) collective-permute-start(bf16[2,128,4,128]{3,1,2,0:T(8,128)(2,1)} %copy.144), channel_id=1, source_target_pairs={{0,4},{4,8},{8,12},{12,16},{16,20},{20,24},{24,28},{28,32},{32,36}... | collective-permute-start | bytes 786440 | tf_op jit(solution)/shard_map/while/body/eval_jaxpr/ppermute | solution.py:13
  104.7 12.3 %collective-permute-start = (bf16[2,128,4,128]{3,1,2,0:T(8,128)(2,1)}, bf16[2,128,4,128]{3,1,2,0:T(8,128)(2,1)S(1)}, u32[]{:S(2)}, u32[]{:S(2)}) collective-permute-start(bf16[2,128,4,128]{3,1,2,0:T(8,128)(2,1)} %copy.144), channel_id=1, source_target_pairs={{0,4},{4,8},{8,12},{12,16},{16,20},{20,24},{24,28},{28,32},{32,36}... | collective-permute-start | bytes 786440 | tf_op jit(solution)/shard_map/while/body/eval_jaxpr/ppermute | solution.py:13
  117.7 12.0 %collective-permute-start = (bf16[2,128,4,128]{3,1,2,0:T(8,128)(2,1)}, bf16[2,128,4,128]{3,1,2,0:T(8,128)(2,1)S(1)}, u32[]{:S(2)}, u32[]{:S(2)}) collective-permute-start(bf16[2,128,4,128]{3,1,2,0:T(8,128)(2,1)} %copy.144), channel_id=1, source_target_pairs={{0,4},{4,8},{8,12},{12,16},{16,20},{20,24},{24,28},{28,32},{32,36}... | collective-permute-start | bytes 786440 | tf_op jit(solution)/shard_map/while/body/eval_jaxpr/ppermute | solution.py:13
  130.4 11.1 %collective-permute-start = (bf16[2,128,4,128]{3,1,2,0:T(8,128)(2,1)}, bf16[2,128,4,128]{3,1,2,0:T(8,128)(2,1)S(1)}, u32[]{:S(2)}, u32[]{:S(2)}) collective-permute-start(bf16[2,128,4,128]{3,1,2,0:T(8,128)(2,1)} %copy.144), channel_id=1, source_target_pairs={{0,4},{4,8},{8,12},{12,16},{16,20},{20,24},{24,28},{28,32},{32,36}... | collective-permute-start | bytes 786440 | tf_op jit(solution)/shard_map/while/body/eval_jaxpr/ppermute | solution.py:13
  142.2 10.2 %collective-permute-start = (bf16[2,128,4,128]{3,1,2,0:T(8,128)(2,1)}, bf16[2,128,4,128]{3,1,2,0:T(8,128)(2,1)S(1)}, u32[]{:S(2)}, u32[]{:S(2)}) collective-permute-start(bf16[2,128,4,128]{3,1,2,0:T(8,128)(2,1)} %copy.144), channel_id=1, source_target_pairs={{0,4},{4,8},{8,12},{12,16},{16,20},{20,24},{24,28},{28,32},{32,36}... | collective-permute-start | bytes 786440 | tf_op jit(solution)/shard_map/while/body/eval_jaxpr/ppermute | solution.py:13
  174.4 10.6 %collective-permute-start = (bf16[2,128,4,128]{3,1,2,0:T(8,128)(2,1)}, bf16[2,128,4,128]{3,1,2,0:T(8,128)(2,1)S(1)}, u32[]{:S(2)}, u32[]{:S(2)}) collective-permute-start(bf16[2,128,4,128]{3,1,2,0:T(8,128)(2,1)} %copy.144), channel_id=1, source_target_pairs={{0,4},{4,8},{8,12},{12,16},{16,20},{20,24},{24,28},{28,32},{32,36}... | collective-permute-start | bytes 786440 | tf_op jit(solution)/shard_map/while/body/eval_jaxpr/ppermute | solution.py:13
  193.5 20.3 %collective-permute-start.1 = (bf16[2,128,4,128]{3,1,2,0:T(8,128)(2,1)}, bf16[2,128,4,128]{3,1,2,0:T(8,128)(2,1)S(1)}, u32[]{:S(2)}, u32[]{:S(2)}) collective-permute-start(bf16[2,128,4,128]{3,1,2,0:T(8,128)(2,1)} %copy.162), channel_id=1, source_target_pairs={{0,4},{4,8},{8,12},{12,16},{16,20},{20,24},{24,28},{28,32},{32,36}... | collective-permute-start | bytes 786440 | tf_op jit(solution)/shard_map/while/body/eval_jaxpr/ppermute | solution.py:13
  202.1 11.6 %collective-permute-start.2 = (bf16[2,128,4,128]{3,1,2,0:T(8,128)(2,1)}, bf16[2,128,4,128]{3,1,2,0:T(8,128)(2,1)S(1)}, u32[]{:S(2)}, u32[]{:S(2)}) collective-permute-start(bf16[2,128,4,128]{3,1,2,0:T(8,128)(2,1)} %fusion.77), channel_id=1, source_target_pairs={{0,4},{4,8},{8,12},{12,16},{16,20},{20,24},{24,28},{28,32},{32,36}... | collective-permute-start | bytes 786440 | tf_op jit(solution)/shard_map/while/body/eval_jaxpr/ppermute | solution.py:13
  214.5 21.3 %collective-permute-start.1 = (bf16[2,128,4,128]{3,1,2,0:T(8,128)(2,1)}, bf16[2,128,4,128]{3,1,2,0:T(8,128)(2,1)S(1)}, u32[]{:S(2)}, u32[]{:S(2)}) collective-permute-start(bf16[2,128,4,128]{3,1,2,0:T(8,128)(2,1)} %copy.162), channel_id=1, source_target_pairs={{0,4},{4,8},{8,12},{12,16},{16,20},{20,24},{24,28},{28,32},{32,36}... | collective-permute-start | bytes 786440 | tf_op jit(solution)/shard_map/while/body/eval_jaxpr/ppermute | solution.py:13
  223.1 12.6 %collective-permute-start.2 = (bf16[2,128,4,128]{3,1,2,0:T(8,128)(2,1)}, bf16[2,128,4,128]{3,1,2,0:T(8,128)(2,1)S(1)}, u32[]{:S(2)}, u32[]{:S(2)}) collective-permute-start(bf16[2,128,4,128]{3,1,2,0:T(8,128)(2,1)} %fusion.77), channel_id=1, source_target_pairs={{0,4},{4,8},{8,12},{12,16},{16,20},{20,24},{24,28},{28,32},{32,36}... | collective-permute-start | bytes 786440 | tf_op jit(solution)/shard_map/while/body/eval_jaxpr/ppermute | solution.py:13
  236.5 20.4 %collective-permute-start.1 = (bf16[2,128,4,128]{3,1,2,0:T(8,128)(2,1)}, bf16[2,128,4,128]{3,1,2,0:T(8,128)(2,1)S(1)}, u32[]{:S(2)}, u32[]{:S(2)}) collective-permute-start(bf16[2,128,4,128]{3,1,2,0:T(8,128)(2,1)} %copy.162), channel_id=1, source_target_pairs={{0,4},{4,8},{8,12},{12,16},{16,20},{20,24},{24,28},{28,32},{32,36}... | collective-permute-start | bytes 786440 | tf_op jit(solution)/shard_map/while/body/eval_jaxpr/ppermute | solution.py:13
  245.1 11.8 %collective-permute-start.2 = (bf16[2,128,4,128]{3,1,2,0:T(8,128)(2,1)}, bf16[2,128,4,128]{3,1,2,0:T(8,128)(2,1)S(1)}, u32[]{:S(2)}, u32[]{:S(2)}) collective-permute-start(bf16[2,128,4,128]{3,1,2,0:T(8,128)(2,1)} %fusion.77), channel_id=1, source_target_pairs={{0,4},{4,8},{8,12},{12,16},{16,20},{20,24},{24,28},{28,32},{32,36}... | collective-permute-start | bytes 786440 | tf_op jit(solution)/shard_map/while/body/eval_jaxpr/ppermute | solution.py:13
  257.6 19.6 %collective-permute-start.1 = (bf16[2,128,4,128]{3,1,2,0:T(8,128)(2,1)}, bf16[2,128,4,128]{3,1,2,0:T(8,128)(2,1)S(1)}, u32[]{:S(2)}, u32[]{:S(2)}) collective-permute-start(bf16[2,128,4,128]{3,1,2,0:T(8,128)(2,1)} %copy.162), channel_id=1, source_target_pairs={{0,4},{4,8},{8,12},{12,16},{16,20},{20,24},{24,28},{28,32},{32,36}... | collective-permute-start | bytes 786440 | tf_op jit(solution)/shard_map/while/body/eval_jaxpr/ppermute | solution.py:13
  261.1 16.0 %collective-permute-start.2 = (bf16[2,128,4,128]{3,1,2,0:T(8,128)(2,1)}, bf16[2,128,4,128]{3,1,2,0:T(8,128)(2,1)S(1)}, u32[]{:S(2)}, u32[]{:S(2)}) collective-permute-start(bf16[2,128,4,128]{3,1,2,0:T(8,128)(2,1)} %fusion.77), channel_id=1, source_target_pairs={{0,4},{4,8},{8,12},{12,16},{16,20},{20,24},{24,28},{28,32},{32,36}... | collective-permute-start | bytes 786440 | tf_op jit(solution)/shard_map/while/body/eval_jaxpr/ppermute | solution.py:13
  277.9 18.6 %collective-permute-start.1 = (bf16[2,128,4,128]{3,1,2,0:T(8,128)(2,1)}, bf16[2,128,4,128]{3,1,2,0:T(8,128)(2,1)S(1)}, u32[]{:S(2)}, u32[]{:S(2)}) collective-permute-start(bf16[2,128,4,128]{3,1,2,0:T(8,128)(2,1)} %copy.162), channel_id=1, source_target_pairs={{0,4},{4,8},{8,12},{12,16},{16,20},{20,24},{24,28},{28,32},{32,36}... | collective-permute-start | bytes 786440 | tf_op jit(solution)/shard_map/while/body/eval_jaxpr/ppermute | solution.py:13
  286.5 10.0 %collective-permute-start.2 = (bf16[2,128,4,128]{3,1,2,0:T(8,128)(2,1)}, bf16[2,128,4,128]{3,1,2,0:T(8,128)(2,1)S(1)}, u32[]{:S(2)}, u32[]{:S(2)}) collective-permute-start(bf16[2,128,4,128]{3,1,2,0:T(8,128)(2,1)} %fusion.77), channel_id=1, source_target_pairs={{0,4},{4,8},{8,12},{12,16},{16,20},{20,24},{24,28},{28,32},{32,36}... | collective-permute-start | bytes 786440 | tf_op jit(solution)/shard_map/while/body/eval_jaxpr/ppermute | solution.py:13
  297.3 18.5 %collective-permute-start.1 = (bf16[2,128,4,128]{3,1,2,0:T(8,128)(2,1)}, bf16[2,128,4,128]{3,1,2,0:T(8,128)(2,1)S(1)}, u32[]{:S(2)}, u32[]{:S(2)}) collective-permute-start(bf16[2,128,4,128]{3,1,2,0:T(8,128)(2,1)} %copy.162), channel_id=1, source_target_pairs={{0,4},{4,8},{8,12},{12,16},{16,20},{20,24},{24,28},{28,32},{32,36}... | collective-permute-start | bytes 786440 | tf_op jit(solution)/shard_map/while/body/eval_jaxpr/ppermute | solution.py:13
  316.6 18.5 %collective-permute-start.1 = (bf16[2,128,4,128]{3,1,2,0:T(8,128)(2,1)}, bf16[2,128,4,128]{3,1,2,0:T(8,128)(2,1)S(1)}, u32[]{:S(2)}, u32[]{:S(2)}) collective-permute-start(bf16[2,128,4,128]{3,1,2,0:T(8,128)(2,1)} %copy.162), channel_id=1, source_target_pairs={{0,4},{4,8},{8,12},{12,16},{16,20},{20,24},{24,28},{28,32},{32,36}... | collective-permute-start | bytes 786440 | tf_op jit(solution)/shard_map/while/body/eval_jaxpr/ppermute | solution.py:13
  335.9 18.5 %collective-permute-start.1 = (bf16[2,128,4,128]{3,1,2,0:T(8,128)(2,1)}, bf16[2,128,4,128]{3,1,2,0:T(8,128)(2,1)S(1)}, u32[]{:S(2)}, u32[]{:S(2)}) collective-permute-start(bf16[2,128,4,128]{3,1,2,0:T(8,128)(2,1)} %copy.162), channel_id=1, source_target_pairs={{0,4},{4,8},{8,12},{12,16},{16,20},{20,24},{24,28},{28,32},{32,36}... | collective-permute-start | bytes 786440 | tf_op jit(solution)/shard_map/while/body/eval_jaxpr/ppermute | solution.py:13
  355.1 18.5 %collective-permute-start.1 = (bf16[2,128,4,128]{3,1,2,0:T(8,128)(2,1)}, bf16[2,128,4,128]{3,1,2,0:T(8,128)(2,1)S(1)}, u32[]{:S(2)}, u32[]{:S(2)}) collective-permute-start(bf16[2,128,4,128]{3,1,2,0:T(8,128)(2,1)} %copy.162), channel_id=1, source_target_pairs={{0,4},{4,8},{8,12},{12,16},{16,20},{20,24},{24,28},{28,32},{32,36}... | collective-permute-start | bytes 786440 | tf_op jit(solution)/shard_map/while/body/eval_jaxpr/ppermute | solution.py:13
  374.4 18.5 %collective-permute-start.1 = (bf16[2,128,4,128]{3,1,2,0:T(8,128)(2,1)}, bf16[2,128,4,128]{3,1,2,0:T(8,128)(2,1)S(1)}, u32[]{:S(2)}, u32[]{:S(2)}) collective-permute-start(bf16[2,128,4,128]{3,1,2,0:T(8,128)(2,1)} %copy.162), channel_id=1, source_target_pairs={{0,4},{4,8},{8,12},{12,16},{16,20},{20,24},{24,28},{28,32},{32,36}... | collective-permute-start | bytes 786440 | tf_op jit(solution)/shard_map/while/body/eval_jaxpr/ppermute | solution.py:13
  393.7 18.5 %collective-permute-start.1 = (bf16[2,128,4,128]{3,1,2,0:T(8,128)(2,1)}, bf16[2,128,4,128]{3,1,2,0:T(8,128)(2,1)S(1)}, u32[]{:S(2)}, u32[]{:S(2)}) collective-permute-start(bf16[2,128,4,128]{3,1,2,0:T(8,128)(2,1)} %copy.162), channel_id=1, source_target_pairs={{0,4},{4,8},{8,12},{12,16},{16,20},{20,24},{24,28},{28,32},{32,36}... | collective-permute-start | bytes 786440 | tf_op jit(solution)/shard_map/while/body/eval_jaxpr/ppermute | solution.py:13
  413.0 18.5 %collective-permute-start.1 = (bf16[2,128,4,128]{3,1,2,0:T(8,128)(2,1)}, bf16[2,128,4,128]{3,1,2,0:T(8,128)(2,1)S(1)}, u32[]{:S(2)}, u32[]{:S(2)}) collective-permute-start(bf16[2,128,4,128]{3,1,2,0:T(8,128)(2,1)} %copy.162), channel_id=1, source_target_pairs={{0,4},{4,8},{8,12},{12,16},{16,20},{20,24},{24,28},{28,32},{32,36}... | collective-permute-start | bytes 786440 | tf_op jit(solution)/shard_map/while/body/eval_jaxpr/ppermute | solution.py:13
  432.2 18.5 %collective-permute-start.1 = (bf16[2,128,4,128]{3,1,2,0:T(8,128)(2,1)}, bf16[2,128,4,128]{3,1,2,0:T(8,128)(2,1)S(1)}, u32[]{:S(2)}, u32[]{:S(2)}) collective-permute-start(bf16[2,128,4,128]{3,1,2,0:T(8,128)(2,1)} %copy.162), channel_id=1, source_target_pairs={{0,4},{4,8},{8,12},{12,16},{16,20},{20,24},{24,28},{28,32},{32,36}... | collective-permute-start | bytes 786440 | tf_op jit(solution)/shard_map/while/body/eval_jaxpr/ppermute | solution.py:13
  451.5 18.5 %collective-permute-start.1 = (bf16[2,128,4,128]{3,1,2,0:T(8,128)(2,1)}, bf16[2,128,4,128]{3,1,2,0:T(8,128)(2,1)S(1)}, u32[]{:S(2)}, u32[]{:S(2)}) collective-permute-start(bf16[2,128,4,128]{3,1,2,0:T(8,128)(2,1)} %copy.162), channel_id=1, source_target_pairs={{0,4},{4,8},{8,12},{12,16},{16,20},{20,24},{24,28},{28,32},{32,36}... | collective-permute-start | bytes 786440 | tf_op jit(solution)/shard_map/while/body/eval_jaxpr/ppermute | solution.py:13
  470.8 18.5 %collective-permute-start.1 = (bf16[2,128,4,128]{3,1,2,0:T(8,128)(2,1)}, bf16[2,128,4,128]{3,1,2,0:T(8,128)(2,1)S(1)}, u32[]{:S(2)}, u32[]{:S(2)}) collective-permute-start(bf16[2,128,4,128]{3,1,2,0:T(8,128)(2,1)} %copy.162), channel_id=1, source_target_pairs={{0,4},{4,8},{8,12},{12,16},{16,20},{20,24},{24,28},{28,32},{32,36}... | collective-permute-start | bytes 786440 | tf_op jit(solution)/shard_map/while/body/eval_jaxpr/ppermute | solution.py:13
  490.1 18.5 %collective-permute-start.1 = (bf16[2,128,4,128]{3,1,2,0:T(8,128)(2,1)}, bf16[2,128,4,128]{3,1,2,0:T(8,128)(2,1)S(1)}, u32[]{:S(2)}, u32[]{:S(2)}) collective-permute-start(bf16[2,128,4,128]{3,1,2,0:T(8,128)(2,1)} %copy.162), channel_id=1, source_target_pairs={{0,4},{4,8},{8,12},{12,16},{16,20},{20,24},{24,28},{28,32},{32,36}... | collective-permute-start | bytes 786440 | tf_op jit(solution)/shard_map/while/body/eval_jaxpr/ppermute | solution.py:13
  (55 other events, 214.3 us)
where the time goes:
time: 697 us; the launch traced here: 693 us
  waiting for transfers between devices  215 us (31%)
  blocking collectives  174 us (25%)
  matrix products  105 us (15%)
  other arithmetic  103 us (15%)
  local copies, waits for them, and re-layouts  54.2 us (8%)
  loops' own time  37.8 us (5%)
    ppermute x49, waiting for transfers between devices, passed_along(): lax.ppermute(value, axis, [(i, (i + by) % size) for i in range(size)])  215 us
    psum x1, blocking collectives, on_device(): summed_table = lax.psum(partial_value, ('ctx', 'dp'))  174 us
    add x16, other arithmetic, backward_turn(): query_sum = query_sum + query_part  37.1 us
    dot_general x15, matrix products, visit(): jnp.einsum('hgqk,khd->qhgd', weights.astype(jnp.bfloat16), block_pair[1],...  22.7 us
    while x31, local copies, waits for them, and re-layouts  22 us
    dot_general x15, matrix products, visit_back(): jnp.einsum('qhgd,khd->hgqk', grouped_queries, block_pair[0], preferred_el...  18.9 us
    dot_general x15, matrix products, visit_back(): jnp.einsum('hgqk,khd->qhgd', score_grad, block_pair[0], preferred_element...  18.9 us
    another operation x1, loops' own time, on_device(): lax.fori_loop(0, cycle_size, backward_turn, (empty_query, key_value, empt...  18.4 us
  transfers between devices with their start and end apart: 49, of which 31 were waited for; matrix products, arithmetic and copies ran while one was open for 32% of the time, Pallas kernels for 0%

commit v1 on v0

--- a/solution.py
+++ b/solution.py
@@ -225,7 +225,7 @@
     )
     log_gradient = -jnp.sum(angle_sums * angles, axis=0)
     partial_value = jnp.dot(log_gradient, onehot, precision=lax.Precision.HIGHEST)
-    summed_table = lax.psum(partial_value, ("ctx", "dp"))
+    summed_table = lax.psum(lax.psum(partial_value, "ctx"), "dp")
     table_grad = summed_table / (cycle_size * lax.axis_size("dp") * tok_rows)
     return (
         final_result.reshape(1, 1, tok_rows, q_width),

time: 697 us -> 573 us (0.82)
  blocking collectives: 174 us -> 47.2 us
    psum x1 -> x2, blocking collectives: 174 us -> 47.2 us  [on_device(): summed_table = lax.psum(lax.psum(partial_value, 'ctx'), 'dp')]
  transfers between devices with their start and end apart: 49 -> 49, of which waited for: 31 -> 31; matrix products, arithmetic and copies ran while one was open for 32% -> 39% of each run, Pallas kernels for 0% -> 0%
where the time goes in v1:
time: 573 us; the launch traced here: 569 us
  waiting for transfers between devices  213 us (37%)
  other arithmetic  105 us (18%)
  matrix products  105 us (18%)
  local copies, waits for them, and re-layouts  54.6 us (10%)
  blocking collectives  47.2 us (8%)
  loops' own time  40.9 us (7%)
    ppermute x49, waiting for transfers between devices, passed_along(): lax.ppermute(value, axis, [(i, (i + by) % size) for i in range(size)])  213 us
    psum x2, blocking collectives, on_device(): summed_table = lax.psum(lax.psum(partial_value, 'ctx'), 'dp')  47.2 us
    add x16, other arithmetic, backward_turn(): query_sum = query_sum + query_part  37 us
    dot_general x15, matrix products, visit(): jnp.einsum('hgqk,khd->qhgd', weights.astype(jnp.bfloat16), block_pair[1],...  22.7 us
    while x31, local copies, waits for them, and re-layouts  21.8 us
    another operation x1, loops' own time, on_device(): lax.fori_loop(0, cycle_size, backward_turn, (empty_query, key_value, empt...  19.9 us
    another operation x1, loops' own time, on_device(): lax.fori_loop(0, cycle_size - 1, forward_turn, (initial, key_value))  19.2 us
    dot_general x15, matrix products, visit_back(): jnp.einsum('qhgd,khd->hgqk', grouped_queries, block_pair[0], preferred_el...  18.9 us
  transfers between devices with their start and end apart: 49, of which 31 were waited for; matrix products, arithmetic and copies ran while one was open for 39% of the time, Pallas kernels for 0%

profile of v1, /device:TPU:0, one launch (start us, length us, event | category | flops | bytes accessed | tf_op | source)
XLA Modules:
  0.0 569.4 jit_solution(12524177019040615482)
XLA Ops:
  14.0 170.8 %while.42 = (s32[]{:T(128)}, f32[4,4,128]{2,1,0:T(4,128)S(1)}, f32[4,4,128]{2,1,0:T(4,128)S(1)}, f32[128,4,4,128]{3,0,2,1:T(8,128)S(1)}, bf16[2,128,4,128]{3,1,2...) while((s32[]{:T(128)}, f32[4,4,128]{2,1,0:T(4,128)S(1)}, ...), condition=%wide.region_8.9_spmd.clone, body=%wide.region_2.8_spmd.clone.sunk | while | flops 137124752 | bytes 7803410 | solution.py:187
  33.0 5.6 collective-permute-done
  52.5 7.7 %collective-permute-done = bf16[2,128,4,128]{3,1,2,0:T(8,128)(2,1)S(1)} collective-permute-done((bf16[2,128,4,128]{3,1,2,0:T(8,128)(2,1)}, bf16[2,128,4,128]{3,1,2,0:T(8,128)(2,1)S(1)}, u32[]{:S(2)}, u32[]{:S(2)}) %collective-permute-start) | collective-permute-done | bytes 262176 | tf_op jit(solution)/shard_map/while/body/eval_jaxpr/ppermute | solution.py:13
  98.3 5.5 collective-permute-done
  110.1 6.7 %collective-permute-done = bf16[2,128,4,128]{3,1,2,0:T(8,128)(2,1)S(1)} collective-permute-done((bf16[2,128,4,128]{3,1,2,0:T(8,128)(2,1)}, bf16[2,128,4,128]{3,1,2,0:T(8,128)(2,1)S(1)}, u32[]{:S(2)}, u32[]{:S(2)}) %collective-permute-start) | collective-permute-done | bytes 262176 | tf_op jit(solution)/shard_map/while/body/eval_jaxpr/ppermute | solution.py:13
  123.2 6.4 %collective-permute-done = bf16[2,128,4,128]{3,1,2,0:T(8,128)(2,1)S(1)} collective-permute-done((bf16[2,128,4,128]{3,1,2,0:T(8,128)(2,1)}, bf16[2,128,4,128]{3,1,2,0:T(8,128)(2,1)S(1)}, u32[]{:S(2)}, u32[]{:S(2)}) %collective-permute-start) | collective-permute-done | bytes 262176 | tf_op jit(solution)/shard_map/while/body/eval_jaxpr/ppermute | solution.py:13
  135.8 5.6 collective-permute-done
  192.6 319.0 %while.43 = (s32[]{:T(128)}, f32[128,4,4,128]{3,0,2,1:T(8,128)}, bf16[2,128,4,128]{3,1,2,0:T(8,128)(2,1)S(1)}, f32[2,128,4,128]{3,1,2,0:T(8,128)S(1)}, s32[]{:T(...) while((s32[]{:T(128)}, f32[128,4,4,128]{3,0,2,1:T(8,128)}, ...), condition=%wide.region_18.19_spmd.clone, body=%wide.region_14.0_spmd.clone.sunk | while | flops 338576288 | bytes 17750600 | solution.py:215
  203.3 10.2 %collective-permute-done.2 = bf16[2,128,4,128]{3,1,2,0:T(8,128)(2,1)S(1)} collective-permute-done((bf16[2,128,4,128]{3,1,2,0:T(8,128)(2,1)}, bf16[2,128,4,128]{3,1,2,0:T(8,128)(2,1)S(1)}, u32[]{:S(2)}, u32[]{:S(2)}) %collective-permute-start.2) | collective-permute-done | bytes 262176 | tf_op jit(solution)/shard_map/while/body/eval_jaxpr/ppermute | solution.py:13
  225.4 10.1 %collective-permute-done.2 = bf16[2,128,4,128]{3,1,2,0:T(8,128)(2,1)S(1)} collective-permute-done((bf16[2,128,4,128]{3,1,2,0:T(8,128)(2,1)}, bf16[2,128,4,128]{3,1,2,0:T(8,128)(2,1)S(1)}, u32[]{:S(2)}, u32[]{:S(2)}) %collective-permute-start.2) | collective-permute-done | bytes 262176 | tf_op jit(solution)/shard_map/while/body/eval_jaxpr/ppermute | solution.py:13
  247.5 9.5 %collective-permute-done.2 = bf16[2,128,4,128]{3,1,2,0:T(8,128)(2,1)S(1)} collective-permute-done((bf16[2,128,4,128]{3,1,2,0:T(8,128)(2,1)}, bf16[2,128,4,128]{3,1,2,0:T(8,128)(2,1)S(1)}, u32[]{:S(2)}, u32[]{:S(2)}) %collective-permute-start.2) | collective-permute-done | bytes 262176 | tf_op jit(solution)/shard_map/while/body/eval_jaxpr/ppermute | solution.py:13
  263.8 13.8 %collective-permute-done.2 = bf16[2,128,4,128]{3,1,2,0:T(8,128)(2,1)S(1)} collective-permute-done((bf16[2,128,4,128]{3,1,2,0:T(8,128)(2,1)}, bf16[2,128,4,128]{3,1,2,0:T(8,128)(2,1)S(1)}, u32[]{:S(2)}, u32[]{:S(2)}) %collective-permute-start.2) | collective-permute-done | bytes 262176 | tf_op jit(solution)/shard_map/while/body/eval_jaxpr/ppermute | solution.py:13
  289.6 7.7 %collective-permute-done.2 = bf16[2,128,4,128]{3,1,2,0:T(8,128)(2,1)S(1)} collective-permute-done((bf16[2,128,4,128]{3,1,2,0:T(8,128)(2,1)}, bf16[2,128,4,128]{3,1,2,0:T(8,128)(2,1)S(1)}, u32[]{:S(2)}, u32[]{:S(2)}) %collective-permute-start.2) | collective-permute-done | bytes 262176 | tf_op jit(solution)/shard_map/while/body/eval_jaxpr/ppermute | solution.py:13
  309.2 7.5 %collective-permute-done.2 = bf16[2,128,4,128]{3,1,2,0:T(8,128)(2,1)S(1)} collective-permute-done((bf16[2,128,4,128]{3,1,2,0:T(8,128)(2,1)}, bf16[2,128,4,128]{3,1,2,0:T(8,128)(2,1)S(1)}, u32[]{:S(2)}, u32[]{:S(2)}) %collective-permute-start.2) | collective-permute-done | bytes 262176 | tf_op jit(solution)/shard_map/while/body/eval_jaxpr/ppermute | solution.py:13
  328.7 7.5 %collective-permute-done.2 = bf16[2,128,4,128]{3,1,2,0:T(8,128)(2,1)S(1)} collective-permute-done((bf16[2,128,4,128]{3,1,2,0:T(8,128)(2,1)}, bf16[2,128,4,128]{3,1,2,0:T(8,128)(2,1)S(1)}, u32[]{:S(2)}, u32[]{:S(2)}) %collective-permute-start.2) | collective-permute-done | bytes 262176 | tf_op jit(solution)/shard_map/while/body/eval_jaxpr/ppermute | solution.py:13
  339.7 5.3 conditional.9
  348.2 7.5 %collective-permute-done.2 = bf16[2,128,4,128]{3,1,2,0:T(8,128)(2,1)S(1)} collective-permute-done((bf16[2,128,4,128]{3,1,2,0:T(8,128)(2,1)}, bf16[2,128,4,128]{3,1,2,0:T(8,128)(2,1)S(1)}, u32[]{:S(2)}, u32[]{:S(2)}) %collective-permute-start.2) | collective-permute-done | bytes 262176 | tf_op jit(solution)/shard_map/while/body/eval_jaxpr/ppermute | solution.py:13
  359.2 5.3 conditional.9
  367.7 7.5 %collective-permute-done.2 = bf16[2,128,4,128]{3,1,2,0:T(8,128)(2,1)S(1)} collective-permute-done((bf16[2,128,4,128]{3,1,2,0:T(8,128)(2,1)}, bf16[2,128,4,128]{3,1,2,0:T(8,128)(2,1)S(1)}, u32[]{:S(2)}, u32[]{:S(2)}) %collective-permute-start.2) | collective-permute-done | bytes 262176 | tf_op jit(solution)/shard_map/while/body/eval_jaxpr/ppermute | solution.py:13
  378.7 5.3 conditional.9
  387.2 7.5 %collective-permute-done.2 = bf16[2,128,4,128]{3,1,2,0:T(8,128)(2,1)S(1)} collective-permute-done((bf16[2,128,4,128]{3,1,2,0:T(8,128)(2,1)}, bf16[2,128,4,128]{3,1,2,0:T(8,128)(2,1)S(1)}, u32[]{:S(2)}, u32[]{:S(2)}) %collective-permute-start.2) | collective-permute-done | bytes 262176 | tf_op jit(solution)/shard_map/while/body/eval_jaxpr/ppermute | solution.py:13
  398.2 5.3 conditional.9
  406.6 7.5 %collective-permute-done.2 = bf16[2,128,4,128]{3,1,2,0:T(8,128)(2,1)S(1)} collective-permute-done((bf16[2,128,4,128]{3,1,2,0:T(8,128)(2,1)}, bf16[2,128,4,128]{3,1,2,0:T(8,128)(2,1)S(1)}, u32[]{:S(2)}, u32[]{:S(2)}) %collective-permute-start.2) | collective-permute-done | bytes 262176 | tf_op jit(solution)/shard_map/while/body/eval_jaxpr/ppermute | solution.py:13
  417.6 5.3 conditional.9
  426.1 7.5 %collective-permute-done.2 = bf16[2,128,4,128]{3,1,2,0:T(8,128)(2,1)S(1)} collective-permute-done((bf16[2,128,4,128]{3,1,2,0:T(8,128)(2,1)}, bf16[2,128,4,128]{3,1,2,0:T(8,128)(2,1)S(1)}, u32[]{:S(2)}, u32[]{:S(2)}) %collective-permute-start.2) | collective-permute-done | bytes 262176 | tf_op jit(solution)/shard_map/while/body/eval_jaxpr/ppermute | solution.py:13
  437.1 5.3 conditional.9
  445.6 7.5 %collective-permute-done.2 = bf16[2,128,4,128]{3,1,2,0:T(8,128)(2,1)S(1)} collective-permute-done((bf16[2,128,4,128]{3,1,2,0:T(8,128)(2,1)}, bf16[2,128,4,128]{3,1,2,0:T(8,128)(2,1)S(1)}, u32[]{:S(2)}, u32[]{:S(2)}) %collective-permute-start.2) | collective-permute-done | bytes 262176 | tf_op jit(solution)/shard_map/while/body/eval_jaxpr/ppermute | solution.py:13
  465.1 7.5 %collective-permute-done.2 = bf16[2,128,4,128]{3,1,2,0:T(8,128)(2,1)S(1)} collective-permute-done((bf16[2,128,4,128]{3,1,2,0:T(8,128)(2,1)}, bf16[2,128,4,128]{3,1,2,0:T(8,128)(2,1)S(1)}, u32[]{:S(2)}, u32[]{:S(2)}) %collective-permute-start.2) | collective-permute-done | bytes 262176 | tf_op jit(solution)/shard_map/while/body/eval_jaxpr/ppermute | solution.py:13
  484.5 7.5 %collective-permute-done.2 = bf16[2,128,4,128]{3,1,2,0:T(8,128)(2,1)S(1)} collective-permute-done((bf16[2,128,4,128]{3,1,2,0:T(8,128)(2,1)}, bf16[2,128,4,128]{3,1,2,0:T(8,128)(2,1)S(1)}, u32[]{:S(2)}, u32[]{:S(2)}) %collective-permute-start.2) | collective-permute-done | bytes 262176 | tf_op jit(solution)/shard_map/while/body/eval_jaxpr/ppermute | solution.py:13
  504.0 7.5 %collective-permute-done.2 = bf16[2,128,4,128]{3,1,2,0:T(8,128)(2,1)S(1)} collective-permute-done((bf16[2,128,4,128]{3,1,2,0:T(8,128)(2,1)}, bf16[2,128,4,128]{3,1,2,0:T(8,128)(2,1)S(1)}, u32[]{:S(2)}, u32[]{:S(2)}) %collective-permute-start.2) | collective-permute-done | bytes 262176 | tf_op jit(solution)/shard_map/while/body/eval_jaxpr/ppermute | solution.py:13
  517.5 35.5 %psum.14 = f32[16]{0:T(128)S(1)} all-reduce(f32[16]{0:T(128)S(1)} %convolution_bitcast_fusion.6), channel_id=1, replica_groups=mesh['pipe'=2,'ctx'=16,'dp'=4] {'ctx'}, use_global_device_ids=true, to_apply=%region_22.23 | all-reduce | flops 16 | bytes 128 | tf_op jit(solution)/shard_map/psum | solution.py:228
  553.0 11.7 %psum.15 = f32[16]{0:T(128)S(1)} all-reduce(f32[16]{0:T(128)S(1)} %psum.14), channel_id=1, replica_groups=mesh['pipe'=2,'ctx'=16,'dp'=4] {'dp'}, use_global_device_ids=true, to_apply=%region_23.24 | all-reduce | flops 16 | bytes 128 | tf_op jit(solution)/shard_map/psum | solution.py:228
  (701 shorter events, 403.6 us)
Async XLA Ops:
  0.6 10.1 %collective-permute-start.3 = (bf16[1,1,128,2048]{3,2,1,0:T(8,128)(2,1)}, bf16[1,1,128,2048]{3,2,1,0:T(8,128)(2,1)S(1)}, u32[]{:S(2)}, u32[]{:S(2)}) collective-permute-start(bf16[1,1,128,2048]{3,2,1,0:T(8,128)(2,1)} %param.21), channel_id=1, source_target_pairs={{0,64},{64,0},{1,65},{65,1},{2,66},{66,2},{3,67},{67,3},{4,68},{68... | collective-permute-start | bytes 1572872 | tf_op jit(solution)/shard_map/ppermute | solution.py:13
  2.8 186.3 %collective-permute-start.4 = (bf16[1,1,128,2048]{2,3,1,0:T(8,128)(2,1)}, bf16[1,1,128,2048]{2,3,1,0:T(8,128)(2,1)}, u32[]{:S(2)}, u32[]{:S(2)}) collective-permute-start(bf16[1,1,128,2048]{2,3,1,0:T(8,128)(2,1)} %copy.95), channel_id=1, source_target_pairs={{0,64},{64,0},{1,65},{65,1},{2,66},{66,2},{3,67},{67,3},{4,68},{68... | collective-permute-start | bytes 1572872 | tf_op jit(solution)/shard_map/ppermute | solution.py:13
  14.7 12.0 %collective-permute-start = (bf16[2,128,4,128]{3,1,2,0:T(8,128)(2,1)}, bf16[2,128,4,128]{3,1,2,0:T(8,128)(2,1)S(1)}, u32[]{:S(2)}, u32[]{:S(2)}) collective-permute-start(bf16[2,128,4,128]{3,1,2,0:T(8,128)(2,1)} %copy.144), channel_id=1, source_target_pairs={{0,4},{4,8},{8,12},{12,16},{16,20},{20,24},{24,28},{28,32},{32,36}... | collective-permute-start | bytes 786440 | tf_op jit(solution)/shard_map/while/body/eval_jaxpr/ppermute | solution.py:13
  27.4 11.2 %collective-permute-start = (bf16[2,128,4,128]{3,1,2,0:T(8,128)(2,1)}, bf16[2,128,4,128]{3,1,2,0:T(8,128)(2,1)S(1)}, u32[]{:S(2)}, u32[]{:S(2)}) collective-permute-start(bf16[2,128,4,128]{3,1,2,0:T(8,128)(2,1)} %copy.144), channel_id=1, source_target_pairs={{0,4},{4,8},{8,12},{12,16},{16,20},{20,24},{24,28},{28,32},{32,36}... | collective-permute-start | bytes 786440 | tf_op jit(solution)/shard_map/while/body/eval_jaxpr/ppermute | solution.py:13
  39.3 10.3 %collective-permute-start = (bf16[2,128,4,128]{3,1,2,0:T(8,128)(2,1)}, bf16[2,128,4,128]{3,1,2,0:T(8,128)(2,1)S(1)}, u32[]{:S(2)}, u32[]{:S(2)}) collective-permute-start(bf16[2,128,4,128]{3,1,2,0:T(8,128)(2,1)} %copy.144), channel_id=1, source_target_pairs={{0,4},{4,8},{8,12},{12,16},{16,20},{20,24},{24,28},{28,32},{32,36}... | collective-permute-start | bytes 786440 | tf_op jit(solution)/shard_map/while/body/eval_jaxpr/ppermute | solution.py:13
  92.8 11.1 %collective-permute-start = (bf16[2,128,4,128]{3,1,2,0:T(8,128)(2,1)}, bf16[2,128,4,128]{3,1,2,0:T(8,128)(2,1)S(1)}, u32[]{:S(2)}, u32[]{:S(2)}) collective-permute-start(bf16[2,128,4,128]{3,1,2,0:T(8,128)(2,1)} %copy.144), channel_id=1, source_target_pairs={{0,4},{4,8},{8,12},{12,16},{16,20},{20,24},{24,28},{28,32},{32,36}... | collective-permute-start | bytes 786440 | tf_op jit(solution)/shard_map/while/body/eval_jaxpr/ppermute | solution.py:13
  104.6 12.3 %collective-permute-start = (bf16[2,128,4,128]{3,1,2,0:T(8,128)(2,1)}, bf16[2,128,4,128]{3,1,2,0:T(8,128)(2,1)S(1)}, u32[]{:S(2)}, u32[]{:S(2)}) collective-permute-start(bf16[2,128,4,128]{3,1,2,0:T(8,128)(2,1)} %copy.144), channel_id=1, source_target_pairs={{0,4},{4,8},{8,12},{12,16},{16,20},{20,24},{24,28},{28,32},{32,36}... | collective-permute-start | bytes 786440 | tf_op jit(solution)/shard_map/while/body/eval_jaxpr/ppermute | solution.py:13
  117.6 12.0 %collective-permute-start = (bf16[2,128,4,128]{3,1,2,0:T(8,128)(2,1)}, bf16[2,128,4,128]{3,1,2,0:T(8,128)(2,1)S(1)}, u32[]{:S(2)}, u32[]{:S(2)}) collective-permute-start(bf16[2,128,4,128]{3,1,2,0:T(8,128)(2,1)} %copy.144), channel_id=1, source_target_pairs={{0,4},{4,8},{8,12},{12,16},{16,20},{20,24},{24,28},{28,32},{32,36}... | collective-permute-start | bytes 786440 | tf_op jit(solution)/shard_map/while/body/eval_jaxpr/ppermute | solution.py:13
  130.3 11.1 %collective-permute-start = (bf16[2,128,4,128]{3,1,2,0:T(8,128)(2,1)}, bf16[2,128,4,128]{3,1,2,0:T(8,128)(2,1)S(1)}, u32[]{:S(2)}, u32[]{:S(2)}) collective-permute-start(bf16[2,128,4,128]{3,1,2,0:T(8,128)(2,1)} %copy.144), channel_id=1, source_target_pairs={{0,4},{4,8},{8,12},{12,16},{16,20},{20,24},{24,28},{28,32},{32,36}... | collective-permute-start | bytes 786440 | tf_op jit(solution)/shard_map/while/body/eval_jaxpr/ppermute | solution.py:13
  142.1 10.2 %collective-permute-start = (bf16[2,128,4,128]{3,1,2,0:T(8,128)(2,1)}, bf16[2,128,4,128]{3,1,2,0:T(8,128)(2,1)S(1)}, u32[]{:S(2)}, u32[]{:S(2)}) collective-permute-start(bf16[2,128,4,128]{3,1,2,0:T(8,128)(2,1)} %copy.144), channel_id=1, source_target_pairs={{0,4},{4,8},{8,12},{12,16},{16,20},{20,24},{24,28},{28,32},{32,36}... | collective-permute-start | bytes 786440 | tf_op jit(solution)/shard_map/while/body/eval_jaxpr/ppermute | solution.py:13
  174.2 10.6 %collective-permute-start = (bf16[2,128,4,128]{3,1,2,0:T(8,128)(2,1)}, bf16[2,128,4,128]{3,1,2,0:T(8,128)(2,1)S(1)}, u32[]{:S(2)}, u32[]{:S(2)}) collective-permute-start(bf16[2,128,4,128]{3,1,2,0:T(8,128)(2,1)} %copy.144), channel_id=1, source_target_pairs={{0,4},{4,8},{8,12},{12,16},{16,20},{20,24},{24,28},{28,32},{32,36}... | collective-permute-start | bytes 786440 | tf_op jit(solution)/shard_map/while/body/eval_jaxpr/ppermute | solution.py:13
  193.3 20.2 %collective-permute-start.1 = (bf16[2,128,4,128]{3,1,2,0:T(8,128)(2,1)}, bf16[2,128,4,128]{3,1,2,0:T(8,128)(2,1)S(1)}, u32[]{:S(2)}, u32[]{:S(2)}) collective-permute-start(bf16[2,128,4,128]{3,1,2,0:T(8,128)(2,1)} %copy.162), channel_id=1, source_target_pairs={{0,4},{4,8},{8,12},{12,16},{16,20},{20,24},{24,28},{28,32},{32,36}... | collective-permute-start | bytes 786440 | tf_op jit(solution)/shard_map/while/body/eval_jaxpr/ppermute | solution.py:13
  202.1 11.4 %collective-permute-start.2 = (bf16[2,128,4,128]{3,1,2,0:T(8,128)(2,1)}, bf16[2,128,4,128]{3,1,2,0:T(8,128)(2,1)S(1)}, u32[]{:S(2)}, u32[]{:S(2)}) collective-permute-start(bf16[2,128,4,128]{3,1,2,0:T(8,128)(2,1)} %fusion.77), channel_id=1, source_target_pairs={{0,4},{4,8},{8,12},{12,16},{16,20},{20,24},{24,28},{28,32},{32,36}... | collective-permute-start | bytes 786440 | tf_op jit(solution)/shard_map/while/body/eval_jaxpr/ppermute | solution.py:13
  214.3 21.4 %collective-permute-start.1 = (bf16[2,128,4,128]{3,1,2,0:T(8,128)(2,1)}, bf16[2,128,4,128]{3,1,2,0:T(8,128)(2,1)S(1)}, u32[]{:S(2)}, u32[]{:S(2)}) collective-permute-start(bf16[2,128,4,128]{3,1,2,0:T(8,128)(2,1)} %copy.162), channel_id=1, source_target_pairs={{0,4},{4,8},{8,12},{12,16},{16,20},{20,24},{24,28},{28,32},{32,36}... | collective-permute-start | bytes 786440 | tf_op jit(solution)/shard_map/while/body/eval_jaxpr/ppermute | solution.py:13
  223.1 12.5 %collective-permute-start.2 = (bf16[2,128,4,128]{3,1,2,0:T(8,128)(2,1)}, bf16[2,128,4,128]{3,1,2,0:T(8,128)(2,1)S(1)}, u32[]{:S(2)}, u32[]{:S(2)}) collective-permute-start(bf16[2,128,4,128]{3,1,2,0:T(8,128)(2,1)} %fusion.77), channel_id=1, source_target_pairs={{0,4},{4,8},{8,12},{12,16},{16,20},{20,24},{24,28},{28,32},{32,36}... | collective-permute-start | bytes 786440 | tf_op jit(solution)/shard_map/while/body/eval_jaxpr/ppermute | solution.py:13
  236.4 20.7 %collective-permute-start.1 = (bf16[2,128,4,128]{3,1,2,0:T(8,128)(2,1)}, bf16[2,128,4,128]{3,1,2,0:T(8,128)(2,1)S(1)}, u32[]{:S(2)}, u32[]{:S(2)}) collective-permute-start(bf16[2,128,4,128]{3,1,2,0:T(8,128)(2,1)} %copy.162), channel_id=1, source_target_pairs={{0,4},{4,8},{8,12},{12,16},{16,20},{20,24},{24,28},{28,32},{32,36}... | collective-permute-start | bytes 786440 | tf_op jit(solution)/shard_map/while/body/eval_jaxpr/ppermute | solution.py:13
  245.2 11.9 %collective-permute-start.2 = (bf16[2,128,4,128]{3,1,2,0:T(8,128)(2,1)}, bf16[2,128,4,128]{3,1,2,0:T(8,128)(2,1)S(1)}, u32[]{:S(2)}, u32[]{:S(2)}) collective-permute-start(bf16[2,128,4,128]{3,1,2,0:T(8,128)(2,1)} %fusion.77), channel_id=1, source_target_pairs={{0,4},{4,8},{8,12},{12,16},{16,20},{20,24},{24,28},{28,32},{32,36}... | collective-permute-start | bytes 786440 | tf_op jit(solution)/shard_map/while/body/eval_jaxpr/ppermute | solution.py:13
  257.8 19.9 %collective-permute-start.1 = (bf16[2,128,4,128]{3,1,2,0:T(8,128)(2,1)}, bf16[2,128,4,128]{3,1,2,0:T(8,128)(2,1)S(1)}, u32[]{:S(2)}, u32[]{:S(2)}) collective-permute-start(bf16[2,128,4,128]{3,1,2,0:T(8,128)(2,1)} %copy.162), channel_id=1, source_target_pairs={{0,4},{4,8},{8,12},{12,16},{16,20},{20,24},{24,28},{28,32},{32,36}... | collective-permute-start | bytes 786440 | tf_op jit(solution)/shard_map/while/body/eval_jaxpr/ppermute | solution.py:13
  261.4 16.2 %collective-permute-start.2 = (bf16[2,128,4,128]{3,1,2,0:T(8,128)(2,1)}, bf16[2,128,4,128]{3,1,2,0:T(8,128)(2,1)S(1)}, u32[]{:S(2)}, u32[]{:S(2)}) collective-permute-start(bf16[2,128,4,128]{3,1,2,0:T(8,128)(2,1)} %fusion.77), channel_id=1, source_target_pairs={{0,4},{4,8},{8,12},{12,16},{16,20},{20,24},{24,28},{28,32},{32,36}... | collective-permute-start | bytes 786440 | tf_op jit(solution)/shard_map/while/body/eval_jaxpr/ppermute | solution.py:13
  278.4 18.9 %collective-permute-start.1 = (bf16[2,128,4,128]{3,1,2,0:T(8,128)(2,1)}, bf16[2,128,4,128]{3,1,2,0:T(8,128)(2,1)S(1)}, u32[]{:S(2)}, u32[]{:S(2)}) collective-permute-start(bf16[2,128,4,128]{3,1,2,0:T(8,128)(2,1)} %copy.162), channel_id=1, source_target_pairs={{0,4},{4,8},{8,12},{12,16},{16,20},{20,24},{24,28},{28,32},{32,36}... | collective-permute-start | bytes 786440 | tf_op jit(solution)/shard_map/while/body/eval_jaxpr/ppermute | solution.py:13
  287.2 10.1 %collective-permute-start.2 = (bf16[2,128,4,128]{3,1,2,0:T(8,128)(2,1)}, bf16[2,128,4,128]{3,1,2,0:T(8,128)(2,1)S(1)}, u32[]{:S(2)}, u32[]{:S(2)}) collective-permute-start(bf16[2,128,4,128]{3,1,2,0:T(8,128)(2,1)} %fusion.77), channel_id=1, source_target_pairs={{0,4},{4,8},{8,12},{12,16},{16,20},{20,24},{24,28},{28,32},{32,36}... | collective-permute-start | bytes 786440 | tf_op jit(solution)/shard_map/while/body/eval_jaxpr/ppermute | solution.py:13
  298.1 18.7 %collective-permute-start.1 = (bf16[2,128,4,128]{3,1,2,0:T(8,128)(2,1)}, bf16[2,128,4,128]{3,1,2,0:T(8,128)(2,1)S(1)}, u32[]{:S(2)}, u32[]{:S(2)}) collective-permute-start(bf16[2,128,4,128]{3,1,2,0:T(8,128)(2,1)} %copy.162), channel_id=1, source_target_pairs={{0,4},{4,8},{8,12},{12,16},{16,20},{20,24},{24,28},{28,32},{32,36}... | collective-permute-start | bytes 786440 | tf_op jit(solution)/shard_map/while/body/eval_jaxpr/ppermute | solution.py:13
  317.5 18.7 %collective-permute-start.1 = (bf16[2,128,4,128]{3,1,2,0:T(8,128)(2,1)}, bf16[2,128,4,128]{3,1,2,0:T(8,128)(2,1)S(1)}, u32[]{:S(2)}, u32[]{:S(2)}) collective-permute-start(bf16[2,128,4,128]{3,1,2,0:T(8,128)(2,1)} %copy.162), channel_id=1, source_target_pairs={{0,4},{4,8},{8,12},{12,16},{16,20},{20,24},{24,28},{28,32},{32,36}... | collective-permute-start | bytes 786440 | tf_op jit(solution)/shard_map/while/body/eval_jaxpr/ppermute | solution.py:13
  337.0 18.7 %collective-permute-start.1 = (bf16[2,128,4,128]{3,1,2,0:T(8,128)(2,1)}, bf16[2,128,4,128]{3,1,2,0:T(8,128)(2,1)S(1)}, u32[]{:S(2)}, u32[]{:S(2)}) collective-permute-start(bf16[2,128,4,128]{3,1,2,0:T(8,128)(2,1)} %copy.162), channel_id=1, source_target_pairs={{0,4},{4,8},{8,12},{12,16},{16,20},{20,24},{24,28},{28,32},{32,36}... | collective-permute-start | bytes 786440 | tf_op jit(solution)/shard_map/while/body/eval_jaxpr/ppermute | solution.py:13
  356.5 18.7 %collective-permute-start.1 = (bf16[2,128,4,128]{3,1,2,0:T(8,128)(2,1)}, bf16[2,128,4,128]{3,1,2,0:T(8,128)(2,1)S(1)}, u32[]{:S(2)}, u32[]{:S(2)}) collective-permute-start(bf16[2,128,4,128]{3,1,2,0:T(8,128)(2,1)} %copy.162), channel_id=1, source_target_pairs={{0,4},{4,8},{8,12},{12,16},{16,20},{20,24},{24,28},{28,32},{32,36}... | collective-permute-start | bytes 786440 | tf_op jit(solution)/shard_map/while/body/eval_jaxpr/ppermute | solution.py:13
  376.0 18.7 %collective-permute-start.1 = (bf16[2,128,4,128]{3,1,2,0:T(8,128)(2,1)}, bf16[2,128,4,128]{3,1,2,0:T(8,128)(2,1)S(1)}, u32[]{:S(2)}, u32[]{:S(2)}) collective-permute-start(bf16[2,128,4,128]{3,1,2,0:T(8,128)(2,1)} %copy.162), channel_id=1, source_target_pairs={{0,4},{4,8},{8,12},{12,16},{16,20},{20,24},{24,28},{28,32},{32,36}... | collective-permute-start | bytes 786440 | tf_op jit(solution)/shard_map/while/body/eval_jaxpr/ppermute | solution.py:13
  395.4 18.7 %collective-permute-start.1 = (bf16[2,128,4,128]{3,1,2,0:T(8,128)(2,1)}, bf16[2,128,4,128]{3,1,2,0:T(8,128)(2,1)S(1)}, u32[]{:S(2)}, u32[]{:S(2)}) collective-permute-start(bf16[2,128,4,128]{3,1,2,0:T(8,128)(2,1)} %copy.162), channel_id=1, source_target_pairs={{0,4},{4,8},{8,12},{12,16},{16,20},{20,24},{24,28},{28,32},{32,36}... | collective-permute-start | bytes 786440 | tf_op jit(solution)/shard_map/while/body/eval_jaxpr/ppermute | solution.py:13
  414.9 18.7 %collective-permute-start.1 = (bf16[2,128,4,128]{3,1,2,0:T(8,128)(2,1)}, bf16[2,128,4,128]{3,1,2,0:T(8,128)(2,1)S(1)}, u32[]{:S(2)}, u32[]{:S(2)}) collective-permute-start(bf16[2,128,4,128]{3,1,2,0:T(8,128)(2,1)} %copy.162), channel_id=1, source_target_pairs={{0,4},{4,8},{8,12},{12,16},{16,20},{20,24},{24,28},{28,32},{32,36}... | collective-permute-start | bytes 786440 | tf_op jit(solution)/shard_map/while/body/eval_jaxpr/ppermute | solution.py:13
  434.4 18.7 %collective-permute-start.1 = (bf16[2,128,4,128]{3,1,2,0:T(8,128)(2,1)}, bf16[2,128,4,128]{3,1,2,0:T(8,128)(2,1)S(1)}, u32[]{:S(2)}, u32[]{:S(2)}) collective-permute-start(bf16[2,128,4,128]{3,1,2,0:T(8,128)(2,1)} %copy.162), channel_id=1, source_target_pairs={{0,4},{4,8},{8,12},{12,16},{16,20},{20,24},{24,28},{28,32},{32,36}... | collective-permute-start | bytes 786440 | tf_op jit(solution)/shard_map/while/body/eval_jaxpr/ppermute | solution.py:13
  453.9 18.7 %collective-permute-start.1 = (bf16[2,128,4,128]{3,1,2,0:T(8,128)(2,1)}, bf16[2,128,4,128]{3,1,2,0:T(8,128)(2,1)S(1)}, u32[]{:S(2)}, u32[]{:S(2)}) collective-permute-start(bf16[2,128,4,128]{3,1,2,0:T(8,128)(2,1)} %copy.162), channel_id=1, source_target_pairs={{0,4},{4,8},{8,12},{12,16},{16,20},{20,24},{24,28},{28,32},{32,36}... | collective-permute-start | bytes 786440 | tf_op jit(solution)/shard_map/while/body/eval_jaxpr/ppermute | solution.py:13
  473.3 18.7 %collective-permute-start.1 = (bf16[2,128,4,128]{3,1,2,0:T(8,128)(2,1)}, bf16[2,128,4,128]{3,1,2,0:T(8,128)(2,1)S(1)}, u32[]{:S(2)}, u32[]{:S(2)}) collective-permute-start(bf16[2,128,4,128]{3,1,2,0:T(8,128)(2,1)} %copy.162), channel_id=1, source_target_pairs={{0,4},{4,8},{8,12},{12,16},{16,20},{20,24},{24,28},{28,32},{32,36}... | collective-permute-start | bytes 786440 | tf_op jit(solution)/shard_map/while/body/eval_jaxpr/ppermute | solution.py:13
  492.8 18.7 %collective-permute-start.1 = (bf16[2,128,4,128]{3,1,2,0:T(8,128)(2,1)}, bf16[2,128,4,128]{3,1,2,0:T(8,128)(2,1)S(1)}, u32[]{:S(2)}, u32[]{:S(2)}) collective-permute-start(bf16[2,128,4,128]{3,1,2,0:T(8,128)(2,1)} %copy.162), channel_id=1, source_target_pairs={{0,4},{4,8},{8,12},{12,16},{16,20},{20,24},{24,28},{28,32},{32,36}... | collective-permute-start | bytes 786440 | tf_op jit(solution)/shard_map/while/body/eval_jaxpr/ppermute | solution.py:13
  (55 other events, 214.9 us)
